TPU v7x, 128 devices: a whole 4x4x4 slice. The times are simulated.
128 devices in a mesh: dp: 4 (over y_hi, core), ctx: 32 (over x, y_lo, z).
Axes of the slice: x: 4, y: 4 (y_hi: 2, y_lo: 2; y = y_hi * 2 + y_lo), z: 4, core: 2. Of those that a mesh axis runs over, the one named last changes fastest.
Arguments:
- frames: float32 [4, 5120, 1536], P('dp', 'ctx'), may hold values from -6 to 6
- teacher: float32 [4, 1536, 768], P('dp'), may hold values from -0.4082483 to 0.4082483
- student: float32 [4, 1536, 768], P('dp'), may hold values from -0.4082483 to 0.4082483
- decay: float32 [4], P('dp'), may hold values from 0.3 to 0.8
- conv_weight: float32 [16, 96, 1536], replicated, may hold values from -0.15625 to 0.15625
- norm_gain: float32 [1536], replicated, may hold values from 0.1 to 1.9
Outputs:
- layer_out: float32 [4, 5120, 1536], P('dp', 'ctx')
- refreshed: float32 [4, 1536, 768], P('dp')
All inputs are finite; a program needn't handle non-finite values.
Results may differ from a plain program's by a relative error of at most 0.0003.
Values sent between devices are 32-bit elements; how exact they have to be, the bound alone decides.
No kernel may reach another device: no remote copies, remote signals or barrier semaphores. Data moves between devices by JAX's collectives and lax.ppermute only.
A program may use at most 256 MiB of HBM per device.

v0:
```python
import jax
import jax.numpy as jnp
from jax import lax
from jax.sharding import PartitionSpec as P

D = 1536
HEADS = 12
HEAD_DIM = 64
GROUP_CH = 96
KERNEL = 16


HIGH = lax.Precision.HIGHEST


def padded_2(cells, sides, width):
    for axis, dim in sides:
        count = lax.axis_size(axis)
        ends = count - 1
        head = lax.slice_in_dim(cells, 0, width, axis=dim)
        tail = lax.slice_in_dim(cells, cells.shape[dim] - width, cells.shape[dim], axis=dim)
        cells = jnp.concatenate(
            [
                lax.ppermute(tail, axis, [(i, (i + 1) % count) for i in range(ends)]),
                cells,
                lax.ppermute(head, axis, [((i + 1) % count, i) for i in range(ends)]),
            ],
            axis=dim,
        )
    return cells


def local(frames, teacher, student, decay, conv_weight, norm_gain):
    refreshed = decay[0] * teacher + (1.0 - decay[0]) * student
    tensors = lax.all_gather(refreshed, "dp", axis=0, tiled=True)
    local_frames = frames.shape[1]
    reach = KERNEL // 2
    padded = padded_2(frames, (("ctx", 1),), reach)
    conv_out = lax.conv_general_dilated(
        padded,
        conv_weight,
        (1,),
        "VALID",
        dimension_numbers=("NWC", "WIO", "NWC"),
        feature_group_count=D // GROUP_CH,
        precision=HIGH,
    )[:, :local_frames]
    mixed = frames + jax.nn.gelu(conv_out, approximate=False)
    center = jnp.mean(mixed, axis=-1, keepdims=True)
    spread_sq = jnp.mean((mixed - center) ** 2, axis=-1, keepdims=True)
    normed = ((mixed - center) / jnp.sqrt(spread_sq + 1e-05) * norm_gain)[0]
    queries = jnp.dot(normed, tensors[0], precision=HIGH)
    key_rows = jnp.dot(normed, tensors[1], precision=HIGH)
    value_rows = jnp.dot(normed, tensors[2], precision=HIGH)
    query_heads = queries.reshape(local_frames, HEADS, HEAD_DIM)
    score_scale = HEAD_DIM ** (-0.5)
    start_weighted = jnp.zeros((local_frames, HEADS * HEAD_DIM), jnp.float32)
    start_max = jnp.full((HEADS, local_frames), -1e30, jnp.float32)
    start_sum = jnp.zeros((HEADS, local_frames), jnp.float32)
    weighted = start_weighted
    key_piece = lax.all_gather(key_rows, "ctx", axis=0, tiled=True)
    value_piece = lax.all_gather(value_rows, "ctx", axis=0, tiled=True)
    count = key_piece.shape[0]
    key_heads = key_piece.reshape(count, HEADS, HEAD_DIM)
    value_heads = value_piece.reshape(count, HEADS, HEAD_DIM)
    scores = jnp.einsum("fhd,phd->hfp", query_heads, key_heads, precision=HIGH) * score_scale
    new_max = jnp.maximum(start_max, jnp.max(scores, axis=-1))
    rescale = jnp.exp(start_max - new_max)
    probs = jnp.exp(scores - new_max[:, :, None])
    new_sum = start_sum * rescale + jnp.sum(probs, axis=-1)
    update = jnp.einsum("hfp,phd->fhd", probs, value_heads, precision=HIGH)
    kept = weighted.reshape(local_frames, HEADS, HEAD_DIM) * rescale.T[:, :, None]
    weighted = (kept + update).reshape(local_frames, HEADS * HEAD_DIM)
    attended = (weighted.reshape(local_frames, HEADS, HEAD_DIM) / new_sum.T[:, :, None]).reshape(
        local_frames, HEADS * HEAD_DIM
    )
    projected = jnp.dot(attended, tensors[3].T, precision=HIGH)
    return (mixed + projected[None], refreshed)


def solution(mesh):
    return jax.shard_map(
        local,
        mesh=mesh,
        in_specs=(
            P("dp", "ctx", None),
            P("dp", None, None),
            P("dp", None, None),
            P("dp"),
            P(),
            P(),
        ),
        out_specs=(P("dp", "ctx", None), P("dp", None, None)),
        check_vma=False,
    )
```

profile of v0, /device:TPU:0, one launch (start us, length us, event | category | flops | bytes accessed | tf_op | source)
XLA Modules:
  0.0 710.4 jit_solution(10956375505091893216)
XLA Ops:
  7.9 6.6 multiply_add_fusion
  14.6 3.9 collective-permute-start
  18.5 1.3 collective-permute-start.1
  19.8 13.1 %shard_map.79 = f32[16,96,16,96]{3,2,1,0:T(8,128)} reshape(f32[16,96,1536]{2,1,0:T(8,128)} %param.10) | data formatting | bytes 18874368 | tf_op jit(solution)/shard_map/shard_map
  32.9 0.1 pad_maximum_fusion
  33.0 4.4 concatenate.6
  37.4 202.0 %fusion.11 = f32[161,16,96]{2,1,0:T(8,128)} fusion(f32[1,176,16,96]{3,0,2,1:T(1,128)} %concatenate.6, f32[16,96,16,96]{3,2,1,0:T(8,128)} %shard_map.79), kind=kOutput, calls=%fused_computation.18 | convolution fusion | flops 4558159872 | bytes 11507712 | tf_op jit(solution)/shard_map/conv_general_dilated | solution.py:39
  239.4 2.0 conv_general_dilated.6
  241.4 2.4 fusion.32
  243.8 0.2 multiply_reduce_fusion.1
  244.1 6.2 fusion.8
  250.3 0.0 all-gather.8.cloned.1.call-start
  250.4 6.2 fusion.7
  256.6 4.8 slice.29
  261.3 6.6 copy.21
  267.9 6.0 fusion.20
  273.9 167.4 %all-gather.6.cloned.1.call-done = f32[5120,768]{1,0:T(8,128)} async-done(((f32[160,768]{1,0:T(8,128)}), f32[5120,768]{1,0:T(8,128)}) %all-gather.6.cloned.1.call-update) | async-done | bytes 15728656 | tf_op jit(solution)/shard_map/all_gather | solution.py:61
  441.3 15.8 %copy.19 = f32[5120,768]{0,1:T(8,128)} copy(f32[5120,768]{1,0:T(8,128)} %all-gather.6.cloned.1.call-done) | data formatting | bytes 31457280 | tf_op jit(solution)/shard_map/all_gather | solution.py:61
  457.0 38.4 %multiply_reduce_fusion = (f32[12,160]{1,0:T(8,128)S(1)}, f32[12,160,5120]{2,1,0:T(8,128)}) fusion(f32[160,12,64]{0,2,1:T(8,128)S(1)} %fusion.20, f32[5120,12,64]{0,2,1:T(8,128)} %bitcast.55), kind=kOutput, calls=%fused_computation.1 | convolution fusion | flops 7569405952 | bytes 55549440 | tf_op jit(solution)/shard_map/fhd,phd->hfp/dot_general | solution.py:66
  495.5 17.0 %fusion = f32[12,160]{1,0:T(8,128)S(1)} fusion(f32[12,160,5120]{2,1,0:T(8,128)} %get-tuple-element.11, f32[12,160]{1,0:T(8,128)S(1)} %get-tuple-element.9), kind=kLoop, calls=%fused_computation.2 | loop fusion | flops 29489280 | bytes 39336960 | tf_op jit(solution)/shard_map/reduce_sum | solution.py:70
  512.5 116.7 %all-gather.8.cloned.1.call-done = f32[5120,768]{1,0:T(8,128)} async-done(((f32[160,768]{1,0:T(8,128)}), f32[5120,768]{1,0:T(8,128)}) %all-gather.8.cloned.1.call-update) | async-done | bytes 15728656 | tf_op jit(solution)/shard_map/all_gather | solution.py:62
  629.2 15.7 %copy.20 = f32[5120,768]{0,1:T(8,128)} copy(f32[5120,768]{1,0:T(8,128)} %all-gather.8.cloned.1.call-done) | data formatting | bytes 31457280 | tf_op jit(solution)/shard_map/all_gather | solution.py:62
  645.0 47.5 %fusion.16 = f32[160,12,64]{0,2,1:T(8,128)S(1)} fusion(f32[5120,12,64]{0,2,1:T(8,128)} %bitcast.54, f32[12,160,5120]{2,1,0:T(8,128)} %get-tuple-element.11, f32[12,160]{1,0:T(8,128)S(1)} %get-tuple-element.9, f32[160,12]{0,1:T(8,128)S(1)} %bitcast_add_fusion, f32[160,12]{0,1:T(8,128)S(1)} %get-tuple-element.8), kind=kOutput, calls=%fused_computation.22 | convolution fusion | flops 7569653760 | bytes 55564800 | tf_op jit(solution)/shard_map/hfp,phd->fhd/dot_general | solution.py:71
  692.5 11.2 %fusion.10 = f32[1,160,1536]{2,1,0:T(8,128)} fusion(f32[1,160,1536]{2,1,0:T(8,128)S(1)} %get-tuple-element.5, f32[160,768]{0,1:T(8,128)S(1)} %bitcast.57, f32[4,1536,768]{2,1,0:T(8,128)} %all-gather.4.cloned.1.call-done), kind=kOutput, calls=%fused_computation.16 | convolution fusion | flops 2265169920 | bytes 7176192 | tf_op jit(solution)/shard_map/dot_general | solution.py:77
  (17 shorter events, 0.2 us)
Async XLA Ops:
  7.2 7.4 %copy-start = (f32[1,160,1536]{2,1,0:T(8,128)S(1)}, f32[1,160,1536]{2,1,0:T(8,128)}, u32[]{:S(2)}) copy-start(f32[1,160,1536]{2,1,0:T(8,128)} %param.6) | copy-start | bytes 2949124
  7.2 236.9 %all-gather.4.cloned.1.call-start = ((), (), s32[]{:S(2)}) async-start(), calls=%async_computation | async-start | bytes 23592960 | tf_op jit(solution)/shard_map/all_gather | solution.py:35
  14.5 426.8 %all-gather.6.cloned.1.call-start = ((), (), s32[]{:S(2)}) async-start(), calls=%async_computation.1 | async-start | bytes 16220160 | tf_op jit(solution)/shard_map/all_gather | solution.py:61
  14.6 18.3 %collective-permute-start = (f32[1,8,1536]{2,1,0:T(8,128)S(1)}, f32[1,8,1536]{2,1,0:T(8,128)S(1)}, u32[]{:S(2)}, u32[]{:S(2)}) collective-permute-start(f32[1,8,1536]{2,1,0:T(8,128)S(1)} %get-tuple-element.6), channel_id=1, source_target_pairs={{0,1},{1,2},{2,3},{3,4},{4,5},{5,6},{6,7},{7,8},{8,9},{9,10},{10,1... | collective-permute-start | bytes 147464 | tf_op jit(solution)/shard_map/ppermute | solution.py:24
  18.5 14.4 %collective-permute-start.1 = (f32[1,8,1536]{2,1,0:T(8,128)S(1)}, f32[1,8,1536]{2,1,0:T(8,128)S(1)}, u32[]{:S(2)}, u32[]{:S(2)}) collective-permute-start(f32[1,8,1536]{2,1,0:T(8,128)S(1)} %get-tuple-element.7), channel_id=1, source_target_pairs={{1,0},{2,1},{3,2},{4,3},{5,4},{6,5},{7,6},{8,7},{9,8},{10,9},{11,1... | collective-permute-start | bytes 147464 | tf_op jit(solution)/shard_map/ppermute | solution.py:26
  37.4 206.7 %copy-start.1 = (f32[1536]{0:T(1024)S(1)}, f32[1536]{0:T(1024)}, u32[]{:S(2)}) copy-start(f32[1536]{0:T(1024)} %param.11) | copy-start | bytes 18436
  250.3 378.9 %all-gather.8.cloned.1.call-start = ((), (), s32[]{:S(2)}) async-start(), calls=%async_computation.2 | async-start | bytes 16220160 | tf_op jit(solution)/shard_map/all_gather | solution.py:62
Sparse Core Ops, SparseCore 0:
  14.6 126.5 all-gather.3
  250.4 190.7 all-gather.5
  443.5 185.6 all-gather.7
where the time goes:
time: 719 us; the launch traced here: 710 us
  matrix products  318 us (44%)
  waiting for transfers between devices  284 us (39%)
  local copies, waits for them, and re-layouts  62.3 us (9%)
  other arithmetic  26.3 us (4%)
  between operations  14.8 us (2%)
    conv_general_dilated x1, matrix products, local(): lax.conv_general_dilated(padded, conv_weight, (1,), 'VALID', dimension_nu...  202 us
    all_gather x1, waiting for transfers between devices, local(): key_piece = lax.all_gather(key_rows, 'ctx', axis=0, tiled=True)  167 us
    all_gather x1, waiting for transfers between devices, local(): value_piece = lax.all_gather(value_rows, 'ctx', axis=0, tiled=True)  117 us
    dot_general x1, matrix products, local(): update = jnp.einsum('hfp,phd->fhd', probs, value_heads, precision=HIGH)  47.5 us
    dot_general x1, matrix products, local(): jnp.einsum('fhd,phd->hfp', query_heads, key_heads, precision=HIGH)  38.4 us
    reduce_sum x1, other arithmetic, local(): new_sum = start_sum * rescale + jnp.sum(probs, axis=-1)  17 us
    all_gather x1, local copies, waits for them, and re-layouts, local(): key_piece = lax.all_gather(key_rows, 'ctx', axis=0, tiled=True)  15.8 us
    all_gather x1, local copies, waits for them, and re-layouts, local(): value_piece = lax.all_gather(value_rows, 'ctx', axis=0, tiled=True)  15.7 us
  transfers between devices with their start and end apart: 5, of which 2 were waited for; matrix products, arithmetic and copies ran while one was open for 45% of the time, Pallas kernels for 0%

commit v1 on v0

v1 whole, which is shorter than its diff:
```python
import functools

import jax
import jax.numpy as jnp
from jax import lax
from jax.experimental import pallas as pl
from jax.experimental.pallas import tpu as pltpu
from jax.sharding import PartitionSpec as P

D = 1536
HEADS = 12
HEAD_DIM = 64
GROUP_CH = 96
KERNEL = 16
REACH = KERNEL // 2
ROWS = 160
QUAD = 4
COLS = HEADS * HEAD_DIM // QUAD
LOCAL_HEADS = HEADS // QUAD
HALF = D // 2
PACK = 2 * COLS
SPAN = QUAD * ROWS
LOG2E = 1.4426950408889634
MIB = 1 << 20
F32 = jnp.float32
BF16 = jnp.bfloat16
L_AT = HEAD_DIM
M_AT = HEAD_DIM + 1


def params(mib):
    return pltpu.CompilerParams(vmem_limit_bytes=mib * MIB)


def two_terms(value):
    high = value.astype(BF16)
    return high, (value - high.astype(F32)).astype(BF16)


def mm(a, b):
    return jnp.dot(a, b, preferred_element_type=F32)


def mm_nt(a, b):
    return lax.dot_general(a, b, (((1,), (1,)), ((), ())), preferred_element_type=F32)


def refresh_kernel(place, decay, teacher, student, refreshed, part):
    rate = decay[0]
    value = rate * teacher[...] + (1.0 - rate) * student[...]
    refreshed[...] = value
    for g in range(QUAD):
        @pl.when(place[1] == g)
        def _():
            cut = slice(g * COLS, (g + 1) * COLS)
            part[...] = jnp.concatenate([value[0, :, cut], value[1, :, cut]], axis=1)


def refresh(place, decay, teacher, student):
    step = 192
    block = pl.BlockSpec((2, step, 768), lambda i: (0, i, 0))
    smem = pl.BlockSpec(memory_space=pltpu.SMEM)
    refreshed, part = pl.pallas_call(
        refresh_kernel,
        grid=(HALF // step,),
        in_specs=[smem, smem, block, block],
        out_specs=[block, pl.BlockSpec((step, PACK), lambda i: (i, 0))],
        out_shape=[
            jax.ShapeDtypeStruct((2, HALF, 768), F32),
            jax.ShapeDtypeStruct((HALF, PACK), F32),
        ],
        compiler_params=params(24),
        cost_estimate=pl.CostEstimate(flops=4 * D * 768, bytes_accessed=15 * MIB, transcendentals=0),
        name="refresh",
    )(place, decay, teacher.reshape(2, HALF, 768), student.reshape(2, HALF, 768))
    return refreshed.reshape(1, D, 768), part


CONV_COLS = 4 * GROUP_CH


def conv_kernel(x, left, right, weight, gain, mixed, normed, padded, group, taps, rhs):
    step = pl.program_id(0)

    @pl.when(step == 0)
    def _():
        rhs[...] = jnp.zeros_like(rhs)

    padded[0:REACH, :] = left[...]
    padded[REACH:REACH + ROWS, :] = x[...]
    padded[REACH + ROWS:, :] = right[...]
    outs = []
    for q in range(4):
        cut = slice(q * GROUP_CH, (q + 1) * GROUP_CH)
        group[...] = jnp.concatenate(
            [padded[:, cut], jnp.zeros((ROWS + 2 * REACH, 128 - GROUP_CH), F32)], axis=1
        )
        for j in range(KERNEL):
            high, low = two_terms(group[j:j + ROWS, :])
            taps[:, j * 256:j * 256 + 128] = high
            taps[:, j * 256 + 128:j * 256 + 256] = low
            wide = jnp.concatenate(
                [weight[j, :, cut], jnp.zeros((GROUP_CH, 128 - GROUP_CH), F32)], axis=1
            )
            high, low = two_terms(wide)
            for base in (j * 256, j * 256 + 128):
                rhs[base:base + GROUP_CH, 0:128] = high
                rhs[base:base + GROUP_CH, 128:256] = low
        both = mm(taps[...], rhs[...])
        outs.append((both[:, :128] + both[:, 128:])[:, :GROUP_CH])
    conv = jnp.concatenate(outs, axis=1)
    value = x[...] + 0.5 * conv * (1.0 + lax.erf(conv * (0.5 ** 0.5)))
    for s in range(D // CONV_COLS):
        @pl.when(step == s)
        def _():
            mixed[:, s * CONV_COLS:(s + 1) * CONV_COLS] = value

    @pl.when(step == D // CONV_COLS - 1)
    def _():
        whole = mixed[...]
        center = jnp.sum(whole, axis=1, keepdims=True) * (1.0 / D)
        shifted = whole - center
        spread = jnp.sum(shifted * shifted, axis=1, keepdims=True) * (1.0 / D)
        normed[...] = shifted * (1.0 / jnp.sqrt(spread + 1e-5)) * gain[...]


def conv_norm(frames, left, right, weight, gain):
    whole = pl.BlockSpec((ROWS, D), lambda i: (0, 0))
    edge = pl.BlockSpec((REACH, CONV_COLS), lambda i: (0, i))
    return pl.pallas_call(
        conv_kernel,
        grid=(D // CONV_COLS,),
        in_specs=[
            pl.BlockSpec((ROWS, CONV_COLS), lambda i: (0, i)),
            edge,
            edge,
            pl.BlockSpec((KERNEL, GROUP_CH, CONV_COLS), lambda i: (0, 0, i)),
            pl.BlockSpec((1, D), lambda i: (0, 0)),
        ],
        out_specs=[whole, whole],
        out_shape=[jax.ShapeDtypeStruct((ROWS, D), F32)] * 2,
        scratch_shapes=[
            pltpu.VMEM((ROWS + 2 * REACH, CONV_COLS), F32),
            pltpu.VMEM((ROWS + 2 * REACH, 128), F32),
            pltpu.VMEM((ROWS, KERNEL * 256), BF16),
            pltpu.VMEM((KERNEL * 256, 256), BF16),
        ],
        compiler_params=params(40),
        cost_estimate=pl.CostEstimate(flops=10 * 10**9, bytes_accessed=12 * MIB, transcendentals=ROWS * D),
        name="conv_norm",
    )(frames, left, right, weight, gain)


def sort_kernel(place, own, core, cross, both, high, low, out_part):
    dp = place[0]
    parts = (own[...], core[...], cross[...], both[...])

    def tensor(t):
        which = jnp.bitwise_xor(dp, t)
        return jnp.where(
            which == 0, parts[0], jnp.where(which == 1, parts[1], jnp.where(which == 2, parts[2], parts[3]))
        )

    query, key, value = tensor(0), tensor(1), tensor(2)
    out_part[...] = tensor(3)
    gap = jnp.zeros((query.shape[0], 256 - COLS), F32)
    for half in range(2):
        cut = slice(half * COLS, (half + 1) * COLS)
        wide = jnp.concatenate([query[:, cut], gap, key[:, cut], value[:, cut]], axis=1)
        high[half], low[half] = two_terms(wide)


def sort_parts(place, own, core, cross, both):
    step = 96
    block = pl.BlockSpec((step, PACK), lambda i: (i, 0))
    wide = pl.BlockSpec((2, step, 256 + PACK), lambda i: (0, i, 0))
    high, low, out_part = pl.pallas_call(
        sort_kernel,
        grid=(HALF // step,),
        in_specs=[pl.BlockSpec(memory_space=pltpu.SMEM)] + [block] * 4,
        out_specs=[wide, wide, block],
        out_shape=[jax.ShapeDtypeStruct((2, HALF, 256 + PACK), BF16)] * 2
        + [jax.ShapeDtypeStruct((HALF, PACK), F32)],
        compiler_params=params(24),
        cost_estimate=pl.CostEstimate(flops=10**7, bytes_accessed=10 * MIB, transcendentals=0),
        name="sort_parts",
    )(place, own, core, cross, both)
    return high.reshape(D, 256 + PACK), low.reshape(D, 256 + PACK), out_part


def project_kernel(own, left, right, far_a, far_b, high, low, queries, pairs):
    def product(rows):
        rows_high, rows_low = two_terms(rows[...])
        return mm(rows_high, high[...]) + mm(rows_high, low[...]) + mm(rows_low, high[...])

    scale = HEAD_DIM ** (-0.5) * LOG2E
    first = product(own)
    pairs[0:ROWS, :] = first[:, 256:]
    second = product(left)
    pairs[ROWS:2 * ROWS, :] = second[:, 256:]
    third = product(right)
    pairs[2 * ROWS:3 * ROWS, :] = third[:, 256:]
    queries[0:ROWS, :] = jnp.concatenate([first[:, :COLS], third[:, :COLS]], axis=1) * scale
    half = ROWS // 2
    for part, far in enumerate((far_a, far_b)):
        last = product(far)
        at = 3 * ROWS + part * half
        pairs[at:at + half, :] = last[:, 256:]
        at = ROWS + part * half
        queries[at:at + half, :] = (
            jnp.concatenate([second[part * half:(part + 1) * half, :COLS], last[:, :COLS]], axis=1) * scale
        )


def project(own, left, right, far_a, far_b, high, low):
    return pl.pallas_call(
        project_kernel,
        out_shape=[
            jax.ShapeDtypeStruct((SPAN // 2, PACK), F32),
            jax.ShapeDtypeStruct((SPAN, PACK), F32),
        ],
        compiler_params=params(40),
        cost_estimate=pl.CostEstimate(flops=6 * SPAN * D * 640, bytes_accessed=10 * MIB, transcendentals=0),
        name="project",
    )(own, left, right, far_a, far_b, high, low)


def doubled(tile, odd):
    lane = lax.broadcasted_iota(jnp.int32, tile.shape, 1)
    turned = pltpu.roll(tile, 64, 1)
    return jnp.where((lane < 64) == (odd == 0), tile, turned)


def chunk(ref, rows, c):
    tile = ref[rows, (c // 2) * 128:(c // 2) * 128 + 128]
    return doubled(tile, c % 2)


def attend_kernel(n_queries, n_blocks, has_state, tile_rows, *refs):
    refs = list(refs)
    query_refs = [refs.pop(0) for _ in range(n_queries)]
    block_refs = [refs.pop(0) for _ in range(n_blocks)]
    state_in = refs.pop(0) if has_state else None
    state, query_cat, key_cat, value_cat = refs
    for n, ref in enumerate(query_refs):
        for half in range(2):
            at = n * SPAN + half * (SPAN // 2)
            for h in range(LOCAL_HEADS):
                value = chunk(ref, slice(None), half * LOCAL_HEADS + h)
                lane = lax.broadcasted_iota(jnp.int32, value.shape, 1)
                high = value.astype(BF16).astype(F32)
                mixture = jnp.where(lane < 64, high, value - high).astype(BF16)
                query_cat[h, at:at + SPAN // 2, 0:128] = mixture
                query_cat[h, at:at + SPAN // 2, 128:256] = mixture
    at = 0
    for ref in block_refs:
        count = ref.shape[0]
        for h in range(LOCAL_HEADS):
            high, low = two_terms(chunk(ref, slice(None), h))
            key_cat[h, at:at + count, 0:128] = high
            key_cat[h, at:at + count, 128:256] = low
            value = chunk(ref, slice(None), LOCAL_HEADS + h)
            lane = lax.broadcasted_iota(jnp.int32, value.shape, 1)
            high = value.astype(BF16).astype(F32)
            low = value - high
            high = jnp.where(lane < 64, high, jnp.where(lane == L_AT, 1.0, 0.0))
            value_cat[h, at:at + count, 0:128] = high.astype(BF16)
            value_cat[h, at:at + count, 128:256] = jnp.where(lane < 64, low, 0.0).astype(BF16)
        at += count
    tiles = n_queries * SPAN // tile_rows

    def body(i, _):
        h = i // tiles
        rows = pl.ds(pl.multiple_of((i % tiles) * tile_rows, tile_rows), tile_rows)
        scores = mm_nt(query_cat[h, rows, :], key_cat[h])
        top = jnp.max(scores, axis=1, keepdims=True)
        if has_state:
            before = state_in[h, rows, :]
            old = before[:, M_AT:M_AT + 1]
            top = jnp.maximum(top, old)
        probs = jnp.exp2(scores - top)
        high, low = two_terms(probs)
        both = mm(high, value_cat[h]) + mm(low, value_cat[h])
        after = both[:, :128] + both[:, 128:]
        if has_state:
            after = after + before * jnp.exp2(old - top)
        lane = lax.broadcasted_iota(jnp.int32, after.shape, 1)
        state[h, rows, :] = jnp.where(lane == M_AT, top, after)
        return 0

    lax.fori_loop(0, LOCAL_HEADS * tiles, body, 0)


def attend(queries, blocks, state=None, tile_rows=320):
    rows = SPAN * len(queries)
    keys = sum(b.shape[0] for b in blocks)
    shape = jax.ShapeDtypeStruct((LOCAL_HEADS, rows, 128), F32)
    operands = list(queries) + list(blocks) + ([] if state is None else [state])
    return pl.pallas_call(
        functools.partial(attend_kernel, len(queries), len(blocks), state is not None, tile_rows),
        out_shape=shape,
        scratch_shapes=[
            pltpu.VMEM((LOCAL_HEADS, rows, 256), BF16),
            pltpu.VMEM((LOCAL_HEADS, keys, 256), BF16),
            pltpu.VMEM((LOCAL_HEADS, keys, 256), BF16),
        ],
        compiler_params=params(48),
        cost_estimate=pl.CostEstimate(
            flops=2 * LOCAL_HEADS * rows * keys * 768, bytes_accessed=6 * MIB, transcendentals=LOCAL_HEADS * rows * keys
        ),
        name="attend",
    )(*operands)


def pack_kernel(state, packed):
    first, second, third = state[0], state[1], state[2]
    lane = lax.broadcasted_iota(jnp.int32, first.shape, 1)
    packed[:, 0:128] = jnp.where(lane < 64, first, pltpu.roll(second, 64, 1))
    packed[:, 128:256] = jnp.where(
        lane < 66, third, jnp.where(lane < 68, pltpu.roll(first, 2, 1), pltpu.roll(second, 4, 1))
    )


def pack(state):
    return pl.pallas_call(
        pack_kernel,
        out_shape=jax.ShapeDtypeStruct((SPAN, 256), F32),
        compiler_params=params(16),
        cost_estimate=pl.CostEstimate(flops=10**6, bytes_accessed=2 * MIB, transcendentals=0),
        name="pack",
    )(state)


def merge_kernel(state, packed, own, left, right, far):
    lane = lax.broadcasted_iota(jnp.int32, (SPAN, 128), 1)
    front, back = packed[:, 0:128], packed[:, 128:256]
    theirs = (
        (front, back[:, 66:67], back[:, 67:68]),
        (pltpu.roll(front, 64, 1), back[:, 68:69], back[:, 69:70]),
        (back, back[:, 64:65], back[:, 65:66]),
    )
    heads = []
    for h in range(LOCAL_HEADS):
        mine = state[h]
        other, other_sum, other_top = theirs[h]
        my_sum, my_top = mine[:, L_AT:L_AT + 1], mine[:, M_AT:M_AT + 1]
        top = jnp.maximum(my_top, other_top)
        a, b = jnp.exp2(my_top - top), jnp.exp2(other_top - top)
        share = 1.0 / (my_sum * a + other_sum * b)
        heads.append(mine * (a * share) + other * (b * share))
    tile = jnp.where(lane < 64, heads[0], pltpu.roll(heads[1], 64, 1))
    attended = jnp.concatenate([tile, heads[2][:, :64]], axis=1)
    half = ROWS // 2
    for s, ref in enumerate((own, left, right, far)):
        at = s * ROWS
        ref[...] = jnp.concatenate([attended[at:at + half], attended[at + half:at + ROWS]], axis=1)


def merge(state, packed):
    return pl.pallas_call(
        merge_kernel,
        out_shape=[jax.ShapeDtypeStruct((ROWS // 2, PACK), F32)] * 4,
        compiler_params=params(24),
        cost_estimate=pl.CostEstimate(flops=10**6, bytes_accessed=2 * MIB, transcendentals=0),
        name="merge",
    )(state, packed)


def output_kernel(mixed, own, left, right, far, part, part_left, part_right, part_far_a, part_far_b, out):
    total = [mixed[:, 0:HALF], mixed[:, HALF:D]]
    for att, parts in (
        (own, (part,)),
        (left, (part_left,)),
        (right, (part_right,)),
        (far, (part_far_a, part_far_b)),
    ):
        rows = jnp.concatenate([att[:, :COLS], att[:, COLS:]], axis=0)
        high, low = two_terms(rows)
        for half in range(2):
            cut = slice(half * COLS, (half + 1) * COLS)
            pieces = []
            for ref in parts:
                part_high, part_low = two_terms(ref[:, cut])
                pieces.append(mm_nt(high, part_high) + mm_nt(high, part_low) + mm_nt(low, part_high))
            total[half] = total[half] + (pieces[0] if len(pieces) == 1 else jnp.concatenate(pieces, axis=1))
    out[:, 0:HALF] = total[0]
    out[:, HALF:D] = total[1]


def output(*operands):
    return pl.pallas_call(
        output_kernel,
        out_shape=jax.ShapeDtypeStruct((ROWS, D), F32),
        compiler_params=params(40),
        cost_estimate=pl.CostEstimate(flops=6 * ROWS * 768 * D, bytes_accessed=8 * MIB, transcendentals=0),
        name="output",
    )(*operands)


def ctx_pairs(dx=0, dy=0, dz=0):
    return [
        ((x * 2 + y) * 4 + z, (((x + dx) % 4) * 2 + (y + dy) % 2) * 4 + (z + dz) % 4)
        for x in range(4)
        for y in range(2)
        for z in range(4)
    ]


def dp_pairs(flip_hi, flip_core):
    pairs = []
    for dp in range(4):
        for ctx in range(32):
            to_dp = dp ^ (2 * flip_hi + flip_core)
            to_ctx = ctx ^ 4 if flip_hi else ctx
            pairs.append((dp * 32 + ctx, to_dp * 32 + to_ctx))
    return pairs


def to_x(value, shift):
    return lax.ppermute(value, "ctx", ctx_pairs(dx=shift))


def to_z(value, shift):
    return lax.ppermute(value, "ctx", ctx_pairs(dz=shift))


def round_ring(move, block):
    before, after = move(block, 1), move(block, -1)
    half = block.shape[0] // 2
    far_a = move(after[:half], -1)
    far_b = move(before[half:], 1)
    return before, after, far_a, far_b


def local(frames, teacher, student, decay, conv_weight, norm_gain):
    dp, ctx = lax.axis_index("dp"), lax.axis_index("ctx")
    place = jnp.stack([dp, ctx // 8]).astype(jnp.int32)
    rows = frames[0]
    left = lax.ppermute(rows[ROWS - REACH:], "ctx", [(i, i + 1) for i in range(31)])
    right = lax.ppermute(rows[:REACH], "ctx", [(i + 1, i) for i in range(31)])

    refreshed, part = refresh(place, decay, teacher, student)
    cross = lax.ppermute(part, ("dp", "ctx"), dp_pairs(1, 0))
    core = lax.ppermute(part, ("dp", "ctx"), dp_pairs(0, 1))
    both = lax.ppermute(cross, ("dp", "ctx"), dp_pairs(0, 1))

    mixed, normed = conv_norm(rows, left, right, conv_weight, norm_gain.reshape(1, D))
    normed_blocks = round_ring(to_x, normed)

    high, low, out_part = sort_parts(place, part, core, cross, both)
    queries, pairs = project(normed, *normed_blocks, high, low)
    partner = lax.ppermute(queries, "ctx", ctx_pairs(dy=1))
    pair_before, pair_after, pair_far_a, pair_far_b = round_ring(to_z, pairs)
    out_blocks = round_ring(to_x, out_part)

    states = []
    for block in ((pairs,), (pair_before, pair_after)):
        states = [
            attend([q], block, None if not states else states[n]) for n, q in enumerate((partner, queries))
        ]
    theirs = attend([partner], (pair_far_a, pair_far_b), states[0])
    packed = lax.ppermute(pack(theirs), "ctx", ctx_pairs(dy=1))
    mine = attend([queries], (pair_far_a, pair_far_b), states[1])

    own, to_before, to_after, to_far = merge(mine, packed)
    from_after = to_x(to_before, -1)
    from_before = to_x(to_after, 1)
    from_far = to_x(to_far, 2)
    out = output(mixed, own, from_before, from_after, from_far, out_part, *out_blocks)
    return out[None], refreshed


def solution(mesh):
    return jax.shard_map(
        local,
        mesh=mesh,
        in_specs=(
            P("dp", "ctx", None),
            P("dp", None, None),
            P("dp", None, None),
            P("dp"),
            P(),
            P(),
        ),
        out_specs=(P("dp", "ctx", None), P("dp", None, None)),
        check_vma=False,
    )
```

time: 719 us -> 181 us (0.25); the launches traced: 710 us -> 181 us
  matrix products: 318 us -> 0 us
  waiting for transfers between devices: 284 us -> 53.5 us
  Pallas kernels: 0 us -> 84.6 us
  local copies, waits for them, and re-layouts: 62.3 us -> 9.4 us
  starting transfers between devices: 5.32 us -> 32 us
  other arithmetic: 26.3 us -> 0.08 us
  between operations: 14.8 us -> 1.55 us
    all_gather x3 -> x0, waiting for transfers between devices: 284 us -> none  [the longest x1 167 us: local(): key_piece = lax.all_gather(key_rows, 'ctx', axis=0, tiled=True)]
    conv_general_dilated x1 -> x0, matrix products: 202 us -> none  [local(): lax.conv_general_dilated(padded, conv_weight, (1,), 'VALID', dimension_nu...]
    dot_general x6 -> x0, matrix products: 116 us -> none  [the longest x1 47.5 us: local(): update = jnp.einsum('hfp,phd->fhd', probs, value_heads, precision=HIGH)]
    pallas_call x0 -> x13, Pallas kernels: none -> 84.6 us  [the longest x6 51.6 us: attend(): pl.pallas_call(functools.partial(attend_kernel, len(queries), len(blocks)...]
    ppermute x2 -> x22, waiting for transfers between devices: 0.01 us -> 53.5 us  [the longest x11 31.7 us: to_x(): return lax.ppermute(value, 'ctx', ctx_pairs(dx=shift))]
    all_gather x2 -> x0, local copies, waits for them, and re-layouts: 31.5 us -> none  [the longest x1 15.8 us: local(): key_piece = lax.all_gather(key_rows, 'ctx', axis=0, tiled=True)]
    ppermute x2 -> x22, starting transfers between devices: 5.2 us -> 32 us  [the longest x11 14.4 us: to_x(): return lax.ppermute(value, 'ctx', ctx_pairs(dx=shift))]
    reduce_sum x3 -> x0, other arithmetic: 19.7 us -> none  [the longest x1 17 us: local(): new_sum = start_sum * rescale + jnp.sum(probs, axis=-1)]
  transfers between devices with their start and end apart: 5 -> 22, of which waited for: 2 -> 8; matrix products, arithmetic and copies ran while one was open for 45% -> 0% of each run, Pallas kernels for 0% -> 41%
where the time goes in v1:
time: 181 us
  Pallas kernels  84.6 us (47%)
  waiting for transfers between devices  53.5 us (30%)
  starting transfers between devices  32 us (18%)
  local copies, waits for them, and re-layouts  9.4 us (5%)
    pallas_call x6, Pallas kernels, attend(): pl.pallas_call(functools.partial(attend_kernel, len(queries), len(blocks)...  51.6 us
    ppermute x11, waiting for transfers between devices, to_x(): return lax.ppermute(value, 'ctx', ctx_pairs(dx=shift))  31.7 us
    ppermute x4, waiting for transfers between devices, to_z(): return lax.ppermute(value, 'ctx', ctx_pairs(dz=shift))  16.8 us
    ppermute x11, starting transfers between devices, to_x(): return lax.ppermute(value, 'ctx', ctx_pairs(dx=shift))  14.4 us
    pallas_call x1, Pallas kernels, conv_norm(): pl.pallas_call(conv_kernel, grid=(D // CONV_COLS,), in_specs=[pl.BlockSpe...  14.1 us
    unnamed x10, local copies, waits for them, and re-layouts  8.35 us
    ppermute x1, starting transfers between devices, local(): cross = lax.ppermute(part, ('dp', 'ctx'), dp_pairs(1, 0))  5.94 us
    pallas_call x1, Pallas kernels, project(): pl.pallas_call(project_kernel, out_shape=[jax.ShapeDtypeStruct((SPAN // 2...  5.62 us
  transfers between devices with their start and end apart: 22, of which 8 were waited for; matrix products, arithmetic and copies ran while one was open for 0% of the time, Pallas kernels for 41%

profile of v1, /device:TPU:0, one launch (start us, length us, event | category | flops | bytes accessed | tf_op | source)
XLA Modules:
  0.0 181.1 jit_solution(3578892124626425833)
XLA Ops:
  1.5 3.9 %collective-permute-start = (f32[8,1536]{1,0:T(8,128)S(1)}, f32[8,1536]{1,0:T(8,128)S(1)}, u32[]{:S(2)}, u32[]{:S(2)}) collective-permute-start(f32[8,1536]{1,0:T(8,128)S(1)} %get-tuple-element.29), channel_id=1, source_target_pairs={{0,1},{1,2},{2,3},{3,4},{4,5},{5,6},{6,7},{7,8},{8,9},{9,10},{10,1... | collective-permute-start | bytes 147464 | tf_op jit(solution)/shard_map/ppermute | solution.py:439
  12.1 3.8 %refresh.1 = (f32[2,768,768]{2,1,0:T(8,128)}, f32[768,384]{1,0:T(8,128)S(1)}) custom-call(s32[2]{0:T(128)S(1)} %pad_add_fusion.place, f32[1]{0:T(128)S(6)} %copy.8.decay, f32[2,768,768]{2,1,0:T(8,128)S(1)} %bitcast.13, f32[2,768,768]{2,1,0:T(8,128)S(1)} %bitcast.14), custom_call_target="tpu_custom_call" | custom-call | flops 4718592 | bytes 15728640 | tf_op jit(solution)/shard_map/refresh/pallas_call | solution.py:63
  15.9 5.9 %collective-permute-start.7 = (f32[768,384]{1,0:T(8,128)S(1)}, f32[768,384]{1,0:T(8,128)S(1)}, u32[]{:S(2)}, u32[]{:S(2)}) collective-permute-start(f32[768,384]{1,0:T(8,128)S(1)} %get-tuple-element.17.own), channel_id=1, source_target_pairs={{0,68},{1,69},{2,70},{3,71},{4,64},{5,65},{6,66},{7,67},{8,76},{9,... | collective-permute-start | bytes 3538952 | tf_op jit(solution)/shard_map/ppermute | solution.py:443
  21.9 3.7 %copy-done.3 = f32[16,96,1536]{2,1,0:T(8,128)S(1)} copy-done((f32[16,96,1536]{2,1,0:T(8,128)S(1)}, f32[16,96,1536]{2,1,0:T(8,128)}, u32[]{:S(2)}) %copy-start.3) | copy-done | bytes 9437208
  25.6 14.1 %conv_norm.1 = (f32[160,1536]{1,0:T(8,128)S(1)}, f32[160,1536]{1,0:T(8,128)S(1)}) custom-call(f32[160,1536]{1,0:T(8,128)S(1)} %bitcast.15, f32[8,1536]{1,0:T(8,128)S(1)} %collective-permute-done.left, f32[8,1536]{1,0:T(8,128)S(1)} %collective-permute-done.1.right, f32[16,96,1536]{2,1,0:T(8,128)S(1)} %copy-done.3, f32[1,1536]{1,0:T(1,128)S(1)} %reshape.24.gain), custom_call_target="tpu_custom_call" | custom-call | flops 10000000000 | bytes 12582912 | tf_op jit(solution)/shard_map/conv_norm/pallas_call | solution.py:130
  39.8 2.9 %collective-permute-start.3 = (f32[160,1536]{1,0:T(8,128)S(1)}, f32[160,1536]{1,0:T(8,128)S(1)}, u32[]{:S(2)}, u32[]{:S(2)}) collective-permute-start(f32[160,1536]{1,0:T(8,128)S(1)} %get-tuple-element.16.own), channel_id=1, source_target_pairs={{0,24},{1,25},{2,26},{3,27},{4,28},{5,29},{6,30},{7,31},{8,0},{9,1... | collective-permute-start | bytes 2949128 | tf_op jit(solution)/shard_map/ppermute | solution.py:420
  42.6 4.9 %collective-permute-done.7.cross = f32[768,384]{1,0:T(8,128)S(1)} collective-permute-done((f32[768,384]{1,0:T(8,128)S(1)}, f32[768,384]{1,0:T(8,128)S(1)}, u32[]{:S(2)}, u32[]{:S(2)}) %collective-permute-start.7) | collective-permute-done | bytes 1179680 | tf_op jit(solution)/shard_map/ppermute | solution.py:443
  47.6 15.5 %collective-permute-done.3.right = f32[160,1536]{1,0:T(8,128)S(1)} collective-permute-done((f32[160,1536]{1,0:T(8,128)S(1)}, f32[160,1536]{1,0:T(8,128)S(1)}, u32[]{:S(2)}, u32[]{:S(2)}) %collective-permute-start.3) | collective-permute-done | bytes 983072 | tf_op jit(solution)/shard_map/ppermute | solution.py:420
  63.1 3.8 %collective-permute-start.4 = (f32[80,1536]{1,0:T(8,128)S(1)}, f32[80,1536]{1,0:T(8,128)S(1)}, u32[]{:S(2)}, u32[]{:S(2)}) collective-permute-start(f32[80,1536]{1,0:T(8,128)S(1)} %slice.40), channel_id=1, source_target_pairs={{0,24},{1,25},{2,26},{3,27},{4,28},{5,29},{6,30},{7,31},{8,0},{9,1... | collective-permute-start | bytes 1474568 | tf_op jit(solution)/shard_map/ppermute | solution.py:420
  67.0 2.5 %sort_parts.1 = (bf16[2,768,640]{2,1,0:T(8,128)(2,1)S(1)}, bf16[2,768,640]{2,1,0:T(8,128)(2,1)S(1)}, f32[768,384]{1,0:T(8,128)S(1)}) custom-call(s32[2]{0:T(128)S(1)} %pad_add_fusion.place, f32[768,384]{1,0:T(8,128)S(1)} %get-tuple-element.17.own, f32[768,384]{1,0:T(8,128)S(1)} %collective-permute-done.6.core, f32[768,384]{1,0:T(8,128)S(1)} %collective-permute-done.7.cross, ...), custom_call_target="tpu_custom_call" | custom-call | flops 10000000 | bytes 10485760 | tf_op jit(solution)/shard_map/sort_parts/pallas_call | solution.py:177
  69.6 6.3 %collective-permute-done.4.far_a = f32[80,1536]{1,0:T(8,128)S(1)} collective-permute-done((f32[80,1536]{1,0:T(8,128)S(1)}, f32[80,1536]{1,0:T(8,128)S(1)}, u32[]{:S(2)}, u32[]{:S(2)}) %collective-permute-start.4) | collective-permute-done | bytes 491552 | tf_op jit(solution)/shard_map/ppermute | solution.py:420
  75.9 3.5 %collective-permute-done.5.far_b = f32[80,1536]{1,0:T(8,128)S(1)} collective-permute-done((f32[80,1536]{1,0:T(8,128)S(1)}, f32[80,1536]{1,0:T(8,128)S(1)}, u32[]{:S(2)}, u32[]{:S(2)}) %collective-permute-start.5) | collective-permute-done | bytes 491552 | tf_op jit(solution)/shard_map/ppermute | solution.py:420
  79.4 5.6 %project.1 = (f32[320,384]{1,0:T(8,128)S(1)}, f32[640,384]{1,0:T(8,128)S(1)}) custom-call(f32[160,1536]{1,0:T(8,128)S(1)} %get-tuple-element.16.own, f32[160,1536]{1,0:T(8,128)S(1)} %collective-permute-done.2.left, f32[160,1536]{1,0:T(8,128)S(1)} %collective-permute-done.3.right, f32[80,1536]{1,0:T(8,128)S(1)} %collective-permute-done.4.far_a, ...), custom_call_target="tpu_custom_call" | custom-call | flops 3774873600 | bytes 10485760 | tf_op jit(solution)/shard_map/project/pallas_call | solution.py:216
  90.3 16.8 %collective-permute-done.9.refs_2_ = f32[640,384]{1,0:T(8,128)S(1)} collective-permute-done((f32[640,384]{1,0:T(8,128)S(1)}, f32[640,384]{1,0:T(8,128)S(1)}, u32[]{:S(2)}, u32[]{:S(2)}) %collective-permute-start.9) | collective-permute-done | bytes 983072 | tf_op jit(solution)/shard_map/ppermute | solution.py:424
  109.3 7.0 %attend.9.refs_3_ = f32[3,640,128]{2,1,0:T(8,128)S(1)} custom-call(f32[320,384]{1,0:T(8,128)S(1)} %collective-permute-done.13.refs_0_, f32[640,384]{1,0:T(8,128)S(1)} %get-tuple-element.21.refs_1_), custom_call_target="tpu_custom_call" | custom-call | flops 1887436800 | bytes 6291456 | tf_op jit(solution)/shard_map/attend/pallas_call | solution.py:299
  116.3 11.0 %attend.10.refs_3_ = f32[3,640,128]{2,1,0:T(8,128)S(1)} custom-call(f32[320,384]{1,0:T(8,128)S(1)} %collective-permute-done.13.refs_0_, f32[640,384]{1,0:T(8,128)S(1)} %collective-permute-done.11.refs_1_, f32[640,384]{1,0:T(8,128)S(1)} %collective-permute-done.9.refs_2_, f32[3,640,128]{2,1,0:T(8,128)S(1)} %attend.9.refs_3_), custom_call_target="tpu_custom_call" | custom-call | flops 3774873600 | bytes 6291456 | tf_op jit(solution)/shard_map/attend/pallas_call | solution.py:299
  127.3 7.8 %attend.11.state = f32[3,640,128]{2,1,0:T(8,128)S(1)} custom-call(f32[320,384]{1,0:T(8,128)S(1)} %collective-permute-done.13.refs_0_, f32[320,384]{1,0:T(8,128)S(1)} %collective-permute-done.10.refs_1_, f32[320,384]{1,0:T(8,128)S(1)} %collective-permute-done.12.refs_2_, f32[3,640,128]{2,1,0:T(8,128)S(1)} %attend.10.refs_3_), custom_call_target="tpu_custom_call" | custom-call | flops 1887436800 | bytes 6291456 | tf_op jit(solution)/shard_map/attend/pallas_call | solution.py:299
  136.6 7.0 %attend.6.refs_3_ = f32[3,640,128]{2,1,0:T(8,128)S(1)} custom-call(f32[320,384]{1,0:T(8,128)S(1)} %get-tuple-element.20.refs_0_, f32[640,384]{1,0:T(8,128)S(1)} %get-tuple-element.21.refs_1_), custom_call_target="tpu_custom_call" | custom-call | flops 1887436800 | bytes 6291456 | tf_op jit(solution)/shard_map/attend/pallas_call | solution.py:299
  146.0 11.0 %attend.7.refs_3_ = f32[3,640,128]{2,1,0:T(8,128)S(1)} custom-call(f32[320,384]{1,0:T(8,128)S(1)} %get-tuple-element.20.refs_0_, f32[640,384]{1,0:T(8,128)S(1)} %collective-permute-done.11.refs_1_, f32[640,384]{1,0:T(8,128)S(1)} %collective-permute-done.9.refs_2_, f32[3,640,128]{2,1,0:T(8,128)S(1)} %attend.6.refs_3_), custom_call_target="tpu_custom_call" | custom-call | flops 3774873600 | bytes 6291456 | tf_op jit(solution)/shard_map/attend/pallas_call | solution.py:299
  157.0 7.8 %attend.8.state = f32[3,640,128]{2,1,0:T(8,128)S(1)} custom-call(f32[320,384]{1,0:T(8,128)S(1)} %get-tuple-element.20.refs_0_, f32[320,384]{1,0:T(8,128)S(1)} %collective-permute-done.10.refs_1_, f32[320,384]{1,0:T(8,128)S(1)} %collective-permute-done.12.refs_2_, f32[3,640,128]{2,1,0:T(8,128)S(1)} %attend.7.refs_3_), custom_call_target="tpu_custom_call" | custom-call | flops 1887436800 | bytes 6291456 | tf_op jit(solution)/shard_map/attend/pallas_call | solution.py:299
  167.4 3.2 %collective-permute-start.16 = (f32[80,384]{1,0:T(8,128)S(1)}, f32[80,384]{1,0:T(8,128)S(1)}, u32[]{:S(2)}, u32[]{:S(2)}) collective-permute-start(f32[80,384]{1,0:T(8,128)S(1)} %get-tuple-element.24), channel_id=1, source_target_pairs={{0,24},{1,25},{2,26},{3,27},{4,28},{5,29},{6,30},{7,31},{8,0},{9,1... | collective-permute-start | bytes 368648 | tf_op jit(solution)/shard_map/ppermute | solution.py:420
  170.6 2.8 %collective-permute-done.15.left = f32[80,384]{1,0:T(8,128)S(1)} collective-permute-done((f32[80,384]{1,0:T(8,128)S(1)}, f32[80,384]{1,0:T(8,128)S(1)}, u32[]{:S(2)}, u32[]{:S(2)}) %collective-permute-start.15) | collective-permute-done | bytes 122912 | tf_op jit(solution)/shard_map/ppermute | solution.py:420
  174.4 2.6 %collective-permute-done.17.far = f32[80,384]{1,0:T(8,128)S(1)} collective-permute-done((f32[80,384]{1,0:T(8,128)S(1)}, f32[80,384]{1,0:T(8,128)S(1)}, u32[]{:S(2)}, u32[]{:S(2)}) %collective-permute-start.17) | collective-permute-done | bytes 122912 | tf_op jit(solution)/shard_map/ppermute | solution.py:420
  177.0 4.1 %output.1 = f32[160,1536]{1,0:T(8,128)} custom-call(f32[160,1536]{1,0:T(8,128)S(1)} %get-tuple-element.15.mixed, f32[80,384]{1,0:T(8,128)S(1)} %get-tuple-element.22.own, f32[80,384]{1,0:T(8,128)S(1)} %collective-permute-done.15.left, f32[80,384]{1,0:T(8,128)S(1)} %collective-permute-done.16.right, f32[80,384]{1,0:T(8,128)S(1)} %collective-permute-done.17.far, ...), custom_call_target="tpu_custom_call" | custom-call | flops 1132462080 | bytes 8388608 | tf_op jit(solution)/shard_map/output/pallas_call | solution.py:391
  (52 shorter events, 21.8 us)
Async XLA Ops:
  1.5 20.4 %collective-permute-start = (f32[8,1536]{1,0:T(8,128)S(1)}, f32[8,1536]{1,0:T(8,128)S(1)}, u32[]{:S(2)}, u32[]{:S(2)}) collective-permute-start(f32[8,1536]{1,0:T(8,128)S(1)} %get-tuple-element.29), channel_id=1, source_target_pairs={{0,1},{1,2},{2,3},{3,4},{4,5},{5,6},{6,7},{7,8},{8,9},{9,10},{10,1... | collective-permute-start | bytes 147464 | tf_op jit(solution)/shard_map/ppermute | solution.py:439
  5.4 16.5 %collective-permute-start.1 = (f32[8,1536]{1,0:T(8,128)S(1)}, f32[8,1536]{1,0:T(8,128)S(1)}, u32[]{:S(2)}, u32[]{:S(2)}) collective-permute-start(f32[8,1536]{1,0:T(8,128)S(1)} %get-tuple-element.28), channel_id=1, source_target_pairs={{1,0},{2,1},{3,2},{4,3},{5,4},{6,5},{7,6},{8,7},{9,8},{10,9},{11,1... | collective-permute-start | bytes 147464 | tf_op jit(solution)/shard_map/ppermute | solution.py:440
  12.1 9.8 %copy-start.4 = (f32[1536]{0:T(1024)S(1)}, f32[1536]{0:T(1024)}, u32[]{:S(2)}) copy-start(f32[1536]{0:T(1024)} %param.11) | copy-start | bytes 18436
  12.1 9.8 %copy-start.2 = (f32[1,160,1536]{2,1,0:T(8,128)S(1)}, f32[1,160,1536]{2,1,0:T(8,128)}, u32[]{:S(2)}) copy-start(f32[1,160,1536]{2,1,0:T(8,128)} %param.6) | copy-start | bytes 2949124
  15.9 31.6 %collective-permute-start.7 = (f32[768,384]{1,0:T(8,128)S(1)}, f32[768,384]{1,0:T(8,128)S(1)}, u32[]{:S(2)}, u32[]{:S(2)}) collective-permute-start(f32[768,384]{1,0:T(8,128)S(1)} %get-tuple-element.17.own), channel_id=1, source_target_pairs={{0,68},{1,69},{2,70},{3,71},{4,64},{5,65},{6,66},{7,67},{8,76},{9,... | collective-permute-start | bytes 3538952 | tf_op jit(solution)/shard_map/ppermute | solution.py:443
  39.8 23.3 %collective-permute-start.3 = (f32[160,1536]{1,0:T(8,128)S(1)}, f32[160,1536]{1,0:T(8,128)S(1)}, u32[]{:S(2)}, u32[]{:S(2)}) collective-permute-start(f32[160,1536]{1,0:T(8,128)S(1)} %get-tuple-element.16.own), channel_id=1, source_target_pairs={{0,24},{1,25},{2,26},{3,27},{4,28},{5,29},{6,30},{7,31},{8,0},{9,1... | collective-permute-start | bytes 2949128 | tf_op jit(solution)/shard_map/ppermute | solution.py:420
  42.6 24.3 %collective-permute-start.2 = (f32[160,1536]{1,0:T(8,128)S(1)}, f32[160,1536]{1,0:T(8,128)S(1)}, u32[]{:S(2)}, u32[]{:S(2)}) collective-permute-start(f32[160,1536]{1,0:T(8,128)S(1)} %get-tuple-element.16.own), channel_id=1, source_target_pairs={{0,8},{1,9},{2,10},{3,11},{4,12},{5,13},{6,14},{7,15},{8,16},{9,17... | collective-permute-start | bytes 2949128 | tf_op jit(solution)/shard_map/ppermute | solution.py:420
  42.6 24.4 %collective-permute-start.6 = (f32[768,384]{1,0:T(8,128)S(1)}, f32[768,384]{1,0:T(8,128)S(1)}, u32[]{:S(2)}, u32[]{:S(2)}) collective-permute-start(f32[768,384]{1,0:T(8,128)S(1)} %get-tuple-element.17.own), channel_id=1, source_target_pairs={{0,32},{1,33},{2,34},{3,35},{4,36},{5,37},{6,38},{7,39},{8,40},{9,... | collective-permute-start | bytes 3538952 | tf_op jit(solution)/shard_map/ppermute | solution.py:444
  47.6 19.4 %collective-permute-start.8 = (f32[768,384]{1,0:T(8,128)S(1)}, f32[768,384]{1,0:T(8,128)S(1)}, u32[]{:S(2)}, u32[]{:S(2)}) collective-permute-start(f32[768,384]{1,0:T(8,128)S(1)} %collective-permute-done.7.cross), channel_id=1, source_target_pairs={{0,32},{1,33},{2,34},{3,35},{4,36},{5,37},{6,38},{7,39},{8,40},{9,... | collective-permute-start | bytes 3538952 | tf_op jit(solution)/shard_map/ppermute | solution.py:445
  63.1 12.8 %collective-permute-start.4 = (f32[80,1536]{1,0:T(8,128)S(1)}, f32[80,1536]{1,0:T(8,128)S(1)}, u32[]{:S(2)}, u32[]{:S(2)}) collective-permute-start(f32[80,1536]{1,0:T(8,128)S(1)} %slice.40), channel_id=1, source_target_pairs={{0,24},{1,25},{2,26},{3,27},{4,28},{5,29},{6,30},{7,31},{8,0},{9,1... | collective-permute-start | bytes 1474568 | tf_op jit(solution)/shard_map/ppermute | solution.py:420
  66.9 12.5 %collective-permute-start.5 = (f32[80,1536]{1,0:T(8,128)S(1)}, f32[80,1536]{1,0:T(8,128)S(1)}, u32[]{:S(2)}, u32[]{:S(2)}) collective-permute-start(f32[80,1536]{1,0:T(8,128)S(1)} %slice.41), channel_id=1, source_target_pairs={{0,8},{1,9},{2,10},{3,11},{4,12},{5,13},{6,14},{7,15},{8,16},{9,17... | collective-permute-start | bytes 1474568 | tf_op jit(solution)/shard_map/ppermute | solution.py:420
  85.0 22.1 %collective-permute-start.9 = (f32[640,384]{1,0:T(8,128)S(1)}, f32[640,384]{1,0:T(8,128)S(1)}, u32[]{:S(2)}, u32[]{:S(2)}) collective-permute-start(f32[640,384]{1,0:T(8,128)S(1)} %get-tuple-element.21.refs_1_), channel_id=1, source_target_pairs={{0,3},{1,0},{2,1},{3,2},{4,7},{5,4},{6,5},{7,6},{8,11},{9,8},{10,9... | collective-permute-start | bytes 2949128 | tf_op jit(solution)/shard_map/ppermute | solution.py:424
  86.6 21.9 %collective-permute-start.11 = (f32[640,384]{1,0:T(8,128)S(1)}, f32[640,384]{1,0:T(8,128)S(1)}, u32[]{:S(2)}, u32[]{:S(2)}) collective-permute-start(f32[640,384]{1,0:T(8,128)S(1)} %get-tuple-element.21.refs_1_), channel_id=1, source_target_pairs={{0,1},{1,2},{2,3},{3,0},{4,5},{5,6},{6,7},{7,4},{8,9},{9,10},{10,1... | collective-permute-start | bytes 2949128 | tf_op jit(solution)/shard_map/ppermute | solution.py:424
  87.3 22.0 %collective-permute-start.13 = (f32[320,384]{1,0:T(8,128)S(1)}, f32[320,384]{1,0:T(8,128)S(1)}, u32[]{:S(2)}, u32[]{:S(2)}) collective-permute-start(f32[320,384]{1,0:T(8,128)S(1)} %get-tuple-element.20.refs_0_), channel_id=1, source_target_pairs={{0,4},{1,5},{2,6},{3,7},{4,0},{5,1},{6,2},{7,3},{8,12},{9,13},{10,... | collective-permute-start | bytes 1474568 | tf_op jit(solution)/shard_map/ppermute | solution.py:452
  88.2 55.3 %collective-permute-start.19 = (f32[768,384]{1,0:T(8,128)S(1)}, f32[768,384]{1,0:T(8,128)S(1)}, u32[]{:S(2)}, u32[]{:S(2)}) collective-permute-start(f32[768,384]{1,0:T(8,128)S(1)} %get-tuple-element.26.part), channel_id=1, source_target_pairs={{0,24},{1,25},{2,26},{3,27},{4,28},{5,29},{6,30},{7,31},{8,0},{9,1... | collective-permute-start | bytes 3538952 | tf_op jit(solution)/shard_map/ppermute | solution.py:420
  88.4 55.4 %collective-permute-start.18 = (f32[768,384]{1,0:T(8,128)S(1)}, f32[768,384]{1,0:T(8,128)S(1)}, u32[]{:S(2)}, u32[]{:S(2)}) collective-permute-start(f32[768,384]{1,0:T(8,128)S(1)} %get-tuple-element.26.part), channel_id=1, source_target_pairs={{0,8},{1,9},{2,10},{3,11},{4,12},{5,13},{6,14},{7,15},{8,16},{9,17... | collective-permute-start | bytes 3538952 | tf_op jit(solution)/shard_map/ppermute | solution.py:420
  107.1 20.2 %collective-permute-start.10 = (f32[320,384]{1,0:T(8,128)S(1)}, f32[320,384]{1,0:T(8,128)S(1)}, u32[]{:S(2)}, u32[]{:S(2)}) collective-permute-start(f32[320,384]{1,0:T(8,128)S(1)} %slice.42), channel_id=1, source_target_pairs={{0,3},{1,0},{2,1},{3,2},{4,7},{5,4},{6,5},{7,6},{8,11},{9,8},{10,9... | collective-permute-start | bytes 1474568 | tf_op jit(solution)/shard_map/ppermute | solution.py:424
  108.5 18.8 %collective-permute-start.12 = (f32[320,384]{1,0:T(8,128)S(1)}, f32[320,384]{1,0:T(8,128)S(1)}, u32[]{:S(2)}, u32[]{:S(2)}) collective-permute-start(f32[320,384]{1,0:T(8,128)S(1)} %slice.43), channel_id=1, source_target_pairs={{0,1},{1,2},{2,3},{3,0},{4,5},{5,6},{6,7},{7,4},{8,9},{9,10},{10,1... | collective-permute-start | bytes 1474568 | tf_op jit(solution)/shard_map/ppermute | solution.py:424
  135.5 29.4 %collective-permute-start.14 = (f32[640,256]{1,0:T(8,128)S(1)}, f32[640,256]{1,0:T(8,128)S(1)}, u32[]{:S(2)}, u32[]{:S(2)}) collective-permute-start(f32[640,256]{1,0:T(8,128)S(1)} %pack.1), channel_id=1, source_target_pairs={{0,4},{1,5},{2,6},{3,7},{4,0},{5,1},{6,2},{7,3},{8,12},{9,13},{10,... | collective-permute-start | bytes 1966088 | tf_op jit(solution)/shard_map/ppermute | solution.py:462
  143.6 27.1 %collective-permute-start.20 = (f32[384,384]{1,0:T(8,128)S(1)}, f32[384,384]{1,0:T(8,128)S(1)}, u32[]{:S(2)}, u32[]{:S(2)}) collective-permute-start(f32[384,384]{1,0:T(8,128)S(1)} %slice.44), channel_id=1, source_target_pairs={{0,24},{1,25},{2,26},{3,27},{4,28},{5,29},{6,30},{7,31},{8,0},{9,1... | collective-permute-start | bytes 1769480 | tf_op jit(solution)/shard_map/ppermute | solution.py:420
  143.9 26.8 %collective-permute-start.21 = (f32[384,384]{1,0:T(8,128)S(1)}, f32[384,384]{1,0:T(8,128)S(1)}, u32[]{:S(2)}, u32[]{:S(2)}) collective-permute-start(f32[384,384]{1,0:T(8,128)S(1)} %slice.45), channel_id=1, source_target_pairs={{0,8},{1,9},{2,10},{3,11},{4,12},{5,13},{6,14},{7,15},{8,16},{9,17... | collective-permute-start | bytes 1769480 | tf_op jit(solution)/shard_map/ppermute | solution.py:420
  167.3 6.2 %collective-permute-start.15 = (f32[80,384]{1,0:T(8,128)S(1)}, f32[80,384]{1,0:T(8,128)S(1)}, u32[]{:S(2)}, u32[]{:S(2)}) collective-permute-start(f32[80,384]{1,0:T(8,128)S(1)} %get-tuple-element.23), channel_id=1, source_target_pairs={{0,8},{1,9},{2,10},{3,11},{4,12},{5,13},{6,14},{7,15},{8,16},{9,17... | collective-permute-start | bytes 368648 | tf_op jit(solution)/shard_map/ppermute | solution.py:420
  167.4 7.0 %collective-permute-start.16 = (f32[80,384]{1,0:T(8,128)S(1)}, f32[80,384]{1,0:T(8,128)S(1)}, u32[]{:S(2)}, u32[]{:S(2)}) collective-permute-start(f32[80,384]{1,0:T(8,128)S(1)} %get-tuple-element.24), channel_id=1, source_target_pairs={{0,24},{1,25},{2,26},{3,27},{4,28},{5,29},{6,30},{7,31},{8,0},{9,1... | collective-permute-start | bytes 368648 | tf_op jit(solution)/shard_map/ppermute | solution.py:420
  170.6 6.4 %collective-permute-start.17 = (f32[80,384]{1,0:T(8,128)S(1)}, f32[80,384]{1,0:T(8,128)S(1)}, u32[]{:S(2)}, u32[]{:S(2)}) collective-permute-start(f32[80,384]{1,0:T(8,128)S(1)} %get-tuple-element.25), channel_id=1, source_target_pairs={{0,16},{1,17},{2,18},{3,19},{4,20},{5,21},{6,22},{7,23},{8,24},{9,... | collective-permute-start | bytes 368648 | tf_op jit(solution)/shard_map/ppermute | solution.py:420
  (3 other events, 8.4 us)
